TPU v7x, 32 devices: a whole 2x2x4 slice. The times are simulated.
32 devices in a mesh: groups: 2 (over y), aa: 4 (over z), ba: 2 (over x), col: 2 (over core).
Axes of the slice: x: 2, y: 2, z: 4, core: 2. Of those that a mesh axis runs over, the one named last changes fastest.
Arguments:
- tokens: bfloat16 [512, 8192], P(('groups', 'col', 'ba'), 'aa'), parts along dimension 0, may hold values from -640 to 640
- norm_gain: bfloat16 [8192], P('aa'), may hold values from 0.099609375 to 1.8984375
- gate_weight: bfloat16 [8192, 14336], P('aa', ('ba', 'col')), may hold values from -0.0625 to 0.0625
- up_weight: bfloat16 [8192, 14336], P('aa', ('ba', 'col')), may hold values from -0.0625 to 0.0625
Outputs:
- hidden: bfloat16 [512, 14336], P(('groups', 'col', 'aa'), 'ba'), parts along dimension 0
There are 2 independent parts, one for each index of `groups`. A program takes and returns all parts, laid end to end along the dimension named above; an argument that names none is the same for every part. Nothing has to cross between parts.
All inputs are finite; a program needn't handle non-finite values.
Results may differ from a plain program's by a relative error of at most 0.015.
Values may be sent and summed in bfloat16 or wider, within the bound.
A program may use at most 192 MiB of HBM per device.

v0:
```python
import jax
import jax.numpy as jnp
from jax import lax
from jax.sharding import PartitionSpec as P

D = 8192


epsilon = 1e-05


def squares(local_rows):
    values = local_rows.astype(jnp.float32)
    return jnp.sum(values * values, axis=1, keepdims=True)


def normalize(local_rows, totals, norm_gain):
    factor = lax.rsqrt(totals / D + epsilon)
    return (local_rows.astype(jnp.float32) * factor * norm_gain.astype(jnp.float32)).astype(
        jnp.bfloat16
    )


def gather_rows(local_rows):
    return lax.all_gather(local_rows, "ba", axis=0, tiled=True)


def make_term(normed, gate_block, up_block):
    gate_part = jnp.dot(normed, gate_block, preferred_element_type=jnp.float32)
    up_part = jnp.dot(normed, up_block, preferred_element_type=jnp.float32)
    return jnp.concatenate([gate_part, up_part], axis=1)


def activate(summed, hidden_units):
    return (jax.nn.silu(summed[:, :hidden_units]) * summed[:, hidden_units:]).astype(jnp.bfloat16)


def shards(tokens, norm_gain, gate_weight, up_weight):
    totals = lax.psum(squares(tokens), "aa")
    normed = gather_rows(normalize(tokens, totals, norm_gain))
    gate_full, up_full = (
        lax.all_gather(gate_weight, "col", axis=1, tiled=True),
        lax.all_gather(up_weight, "col", axis=1, tiled=True),
    )
    summed = lax.psum_scatter(
        make_term(normed, gate_full, up_full).astype(jnp.bfloat16),
        "aa",
        scatter_dimension=0,
        tiled=True,
    ).astype(jnp.float32)
    return activate(summed, gate_full.shape[1])


def solution(mesh):
    return jax.shard_map(
        shards,
        mesh=mesh,
        in_specs=(
            P(("groups", "col", "ba"), "aa"),
            P("aa"),
            P("aa", ("ba", "col")),
            P("aa", ("ba", "col")),
        ),
        out_specs=P(("groups", "col", "aa"), "ba"),
        check_vma=False,
    )
```

profile of v0, /device:TPU:0, one launch (start us, length us, event | category | flops | bytes accessed | tf_op | source)
XLA Modules:
  0.0 202.0 jit_solution(15010037423138820692)
XLA Ops:
  6.5 0.0 all-gather.5.cloned.1.call-start
  6.5 0.7 all-gather.5.cloned.1.call-update
  7.3 0.0 copy-start.1
  7.3 0.0 copy-start
  7.3 0.0 all-gather.3.cloned.1.call-start
  7.3 0.7 all-gather.3.cloned.1.call-update
  8.0 0.0 reduce-scatter.2.cloned.1.call-start
  8.1 0.0 copy-done.1
  8.1 0.1 copy-done
  8.2 0.2 fusion.1
  8.4 13.5 %psum.7 = f32[64,1]{0,1:T(1,128)S(1)} all-reduce(f32[64,1]{0,1:T(1,128)S(1)} %bitcast.7), channel_id=1, replica_groups=mesh['groups'=2,'aa'=4,'ba'=2,'col'=2] {'aa'}, use_global_device_ids=true, to_apply=%region_1.0 | all-reduce | flops 64 | bytes 512 | tf_op jit(solution)/shard_map/psum | solution.py:39
  21.8 0.1 fusion.3
  22.0 7.0 %all_gather.9 = bf16[128,2048]{1,0:T(8,128)(2,1)S(1)} all-gather(bf16[64,2048]{1,0:T(8,128)(2,1)S(1)} %fusion.3), channel_id=1, replica_groups=mesh['groups'=2,'aa'=4,'ba'=2,'col'=2] {'ba'}, dimensions={0}, use_global_device_ids=true | all-gather | bytes 786432 | tf_op jit(solution)/shard_map/all_gather | solution.py:25
  29.0 29.4 %all-gather.5.cloned.1.call-done = bf16[2048,7168]{1,0:T(8,128)(2,1)} async-done(((bf16[2048,3584]{1,0:T(8,128)(2,1)}), bf16[2048,7168]{1,0:T(8,128)(2,1)}) %all-gather.5.cloned.1.call-update) | async-done | bytes 29360144 | tf_op jit(solution)/shard_map/all_gather | solution.py:43
  58.5 13.9 %convolution_convert_fusion = bf16[128,7168]{1,0:T(8,128)(2,1)S(1)} fusion(bf16[128,2048]{1,0:T(8,128)(2,1)S(1)} %all_gather.9, bf16[2048,7168]{1,0:T(8,128)(2,1)} %all-gather.5.cloned.1.call-done), kind=kOutput, calls=%fused_computation | convolution fusion | flops 3759013888 | bytes 31719424 | tf_op jit(solution)/shard_map/dot_general | solution.py:30
  72.4 35.6 %all-gather.3.cloned.1.call-done = bf16[2048,7168]{1,0:T(8,128)(2,1)} async-done(((bf16[2048,3584]{1,0:T(8,128)(2,1)}), bf16[2048,7168]{1,0:T(8,128)(2,1)}) %all-gather.3.cloned.1.call-update) | async-done | bytes 29360144 | tf_op jit(solution)/shard_map/all_gather | solution.py:42
  108.0 13.3 %convolution_convert_fusion.1 = bf16[128,7168]{1,0:T(8,128)(2,1)S(1)} fusion(bf16[128,2048]{1,0:T(8,128)(2,1)S(1)} %all_gather.9, bf16[2048,7168]{1,0:T(8,128)(2,1)} %all-gather.3.cloned.1.call-done), kind=kOutput, calls=%fused_computation.1 | convolution fusion | flops 3759013888 | bytes 31719424 | tf_op jit(solution)/shard_map/dot_general | solution.py:29
  121.3 2.0 %pad_maximum_fusion = bf16[128,14336]{1,0:T(8,128)(2,1)} fusion(bf16[128,7168]{1,0:T(8,128)(2,1)S(1)} %convolution_convert_fusion, bf16[128,7168]{1,0:T(8,128)(2,1)S(1)} %convolution_convert_fusion.1), kind=kLoop, calls=%fused_computation.2 | loop fusion | flops 7340032 | bytes 7340032 | tf_op jit(solution)/shard_map/concatenate | solution.py:31
  123.4 0.0 reduce-scatter.2.cloned.1.call-update
  123.4 69.7 %reduce-scatter.2.cloned.1.call-done = bf16[32,14336]{1,0:T(8,128)(2,1)} async-done(((bf16[128,14336]{1,0:T(8,128)(2,1)}), bf16[32,14336]{1,0:T(8,128)(2,1)}) %reduce-scatter.2.cloned.1.call-update) | async-done | bytes 917520 | tf_op jit(solution)/shard_map/reduce_scatter | solution.py:45
  193.1 1.3 convert_element_type.20
  194.4 1.0 fusion
  (2 shorter events, 0.0 us)
Async XLA Ops:
  6.5 51.9 %all-gather.5.cloned.1.call-start = ((), (), s32[]{:S(2)}) async-start(), calls=%async_computation.2 | async-start | bytes 44040192 | tf_op jit(solution)/shard_map/all_gather | solution.py:43
  7.3 0.8 copy-start.1
  7.3 1.0 copy-start
  7.3 100.7 %all-gather.3.cloned.1.call-start = ((), (), s32[]{:S(2)}) async-start(), calls=%async_computation.1 | async-start | bytes 44040192 | tf_op jit(solution)/shard_map/all_gather | solution.py:42
  8.0 185.1 %reduce-scatter.2.cloned.1.call-start = ((), (), s32[]{:S(2)}) async-start(), calls=%async_computation.3 | async-start | bytes 4587520 | tf_op jit(solution)/shard_map/reduce_scatter | solution.py:45
Sparse Core Ops, SparseCore 0:
  8.9 49.4 all-gather.4
  60.0 47.9 all-gather.2
  123.5 69.5 reduce-scatter.1
where the time goes:
time: 202 us
  waiting for transfers between devices  136 us (67%)
  matrix products  27.2 us (13%)
  blocking collectives  20.5 us (10%)
  between operations  13.2 us (7%)
  other arithmetic  4.66 us (2%)
    reduce_scatter x1, waiting for transfers between devices, shards(): lax.psum_scatter(make_term(normed, gate_full, up_full).astype(jnp.bfloat1...  69.7 us
    all_gather x1, waiting for transfers between devices, shards(): lax.all_gather(gate_weight, 'col', axis=1, tiled=True)  35.6 us
    all_gather x1, waiting for transfers between devices, shards(): lax.all_gather(up_weight, 'col', axis=1, tiled=True)  29.4 us
    dot_general x1, matrix products, make_term(): up_part = jnp.dot(normed, up_block, preferred_element_type=jnp.float32)  13.9 us
    psum x1, blocking collectives, shards(): totals = lax.psum(squares(tokens), 'aa')  13.5 us
    dot_general x1, matrix products, make_term(): gate_part = jnp.dot(normed, gate_block, preferred_element_type=jnp.float32)  13.3 us
    all_gather x1, blocking collectives, gather_rows(): return lax.all_gather(local_rows, 'ba', axis=0, tiled=True)  7.05 us
  transfers between devices with their start and end apart: 3, of which 3 were waited for; matrix products, arithmetic and copies ran while one was open for 7% of the time, Pallas kernels for 0%

commit v1 on v0

v1 whole, which is shorter than its diff:
```python
import functools

import jax
import jax.numpy as jnp
from jax import lax
from jax.experimental import pallas as pl
from jax.experimental.pallas import tpu as pltpu
from jax.sharding import PartitionSpec as P

MESH = pl.DeviceIdType.MESH
EPSILON = 1e-05
LAG = 2


def kernel(sizes, tokens, gain, gate_w, up_w, out, raw, scaled, gate_v, up_v, acc, recv, send,
           hid, sq_own, sq_recv, factor, w_sem, own_sem, x_send, x_recv, c_send, c_recv,
           part_send, part_recv, sq_send, sq_rsem, hid_send, out_recv):
    n, n_ba, n_col, tiles = sizes
    a, b, c = lax.axis_index("aa"), lax.axis_index("ba"), lax.axis_index("col")
    own_rows, depth = tokens.shape
    width = gate_w.shape[1]
    tu = width // tiles
    half = scaled.shape[0] // 2
    out_rows = out.shape[0]
    dests = n // 2

    def start_of(bb, cc):
        per_half = n_ba // 2
        row = (bb // per_half) * half + cc * (half // n_col) + (bb % per_half) * own_rows
        return pl.multiple_of(row, own_rows)

    def block(bb, cc):
        return raw.at[pl.ds(start_of(bb, cc), own_rows)]

    def weight_copies(j):
        cols = pl.ds(pl.multiple_of(j * tu, tu), tu)
        return (pltpu.make_async_copy(gate_w.at[:, cols], gate_v.at[j], w_sem.at[0, j]),
                pltpu.make_async_copy(up_w.at[:, cols], up_v.at[j], w_sem.at[1, j]))

    barrier = pltpu.get_barrier_semaphore()
    peers = 0
    for da in range(n):
        for dc in range(n_col):
            if da or dc:
                pl.semaphore_signal(
                    barrier, inc=1, device_id_type=MESH,
                    device_id={"aa": lax.rem(a + da, n), "col": lax.rem(c + dc, n_col)})
                peers += 1
    for db in range(1, n_ba):
        pl.semaphore_signal(barrier, inc=1, device_id={"ba": lax.rem(b + db, n_ba)},
                            device_id_type=MESH)
        peers += 1

    own = pltpu.make_async_copy(tokens, block(b, c), own_sem)
    own.start()

    @pl.loop(0, tiles)
    def _(j):
        for copy in weight_copies(j):
            copy.start()

    pl.semaphore_wait(barrier, peers)

    def to_chip(db):
        return pltpu.make_async_remote_copy(
            tokens, block(b, c), x_send.at[db], x_recv.at[db],
            device_id={"ba": lax.rem(b + db, n_ba)}, device_id_type=MESH)

    def from_chip(db):
        return pltpu.make_async_remote_copy(
            tokens, block(lax.rem(b - db + n_ba, n_ba), c), x_send.at[db], x_recv.at[db],
            device_id={"ba": lax.rem(b + db, n_ba)}, device_id_type=MESH)

    def to_core(db, dc):
        spot = block(lax.rem(b - db + n_ba, n_ba), c)
        return pltpu.make_async_remote_copy(
            tokens if db == 0 else spot, spot, c_send.at[db, dc], c_recv.at[db, dc],
            device_id={"col": lax.rem(c + dc, n_col)}, device_id_type=MESH)

    def from_core(db, dc):
        spot = block(lax.rem(b - db + n_ba, n_ba), lax.rem(c - dc + n_col, n_col))
        return pltpu.make_async_remote_copy(
            tokens, spot, c_send.at[db, dc], c_recv.at[db, dc],
            device_id={"col": lax.rem(c + dc, n_col)}, device_id_type=MESH)

    for db in range(1, n_ba):
        to_chip(db).start()
    for dc in range(1, n_col):
        to_core(0, dc).start()
    for db in range(1, n_ba):
        from_chip(db).wait_recv()
        for dc in range(1, n_col):
            to_core(db, dc).start()
    own.wait()
    for db in range(n_ba):
        for dc in range(1, n_col):
            from_core(db, dc).wait_recv()

    @pl.loop(0, 2 * half // 128)
    def _(r):
        rows = pl.ds(pl.multiple_of(r * 128, 128), 128)
        total = jnp.zeros((128, 128), jnp.float32)
        for q in range(depth // 128):
            cols = slice(q * 128, (q + 1) * 128)
            value = raw[rows, cols].astype(jnp.float32)
            total = total + value * value
            scaled[rows, cols] = (value * gain[:, cols].astype(jnp.float32)).astype(jnp.bfloat16)
        line = jnp.sum(jnp.transpose(total), axis=0, keepdims=True)
        per = half // 128
        sq_own[r // per, r % per] = jnp.broadcast_to(line, (8, 128))

    def sq_copy(h, slot):
        return pltpu.make_async_remote_copy(
            sq_own.at[h], sq_recv.at[slot], sq_send.at[h], sq_rsem.at[slot],
            device_id={"aa": h * (n - 1)}, device_id_type=MESH)

    for h in range(2):
        @pl.when(a != h * (n - 1))
        def _():
            sq_copy(h, a).start()

    def part_copy(h, k):
        to = jnp.maximum(a - 1, 0) if h == 0 else jnp.minimum(a + 1, n - 1)
        return pltpu.make_async_remote_copy(
            send.at[h, k], recv.at[h, k], part_send.at[h, k], part_recv.at[h, k],
            device_id={"aa": to}, device_id_type=MESH)

    def hid_copy(h, k, dd, cc):
        index = cc * dests + dd
        spot = out.at[:, pl.ds(pl.multiple_of(c * width + k * tu, tu), tu)]
        return pltpu.make_async_remote_copy(
            hid.at[k, pl.ds(index * out_rows, out_rows)], spot,
            hid_send.at[k, index], out_recv.at[k, c],
            device_id={"aa": h * dests + dd, "col": cc}, device_id_type=MESH)

    def mine(h, dd, cc):
        return (c == cc) if dd == h * (dests - 1) else False

    def hop(h):
        return n - 1 - a if h == 0 else a

    def handle(h, k):
        here = hop(h)
        rows = slice(h * half, (h + 1) * half)

        @pl.when(here > 0)
        def _():
            part_copy(h, k).wait_recv()

        @pl.when(here == 0)
        def _():
            send[h, k] = acc[k, rows, :].astype(jnp.bfloat16)

        @pl.when((here > 0) & (here < n - 1))
        def _():
            send[h, k] = (acc[k, rows, :] + recv[h, k].astype(jnp.float32)).astype(jnp.bfloat16)

        @pl.when(here < n - 1)
        def _():
            part_copy(h, k).start()

        @pl.when(here == n - 1)
        def _():
            @pl.when(k == 0)
            def _():
                total = sq_own[h]
                for d in range(n):
                    if d != h * (n - 1):
                        sq_copy(h, d).wait_recv()
                        total = total + sq_recv[d]
                rate = lax.rsqrt(total / (depth * n) + EPSILON)
                for r in range(half // 128):
                    factor[r * 128:(r + 1) * 128, :] = jnp.transpose(
                        jnp.broadcast_to(rate[r, 0:1, :], (128, 128)))

            scale = factor[...]
            for q in range(tu // 128):
                at = slice(q * 128, (q + 1) * 128)
                late = slice(tu + q * 128, tu + (q + 1) * 128)
                gate = (acc[k, rows, at] + recv[h, k, :, at].astype(jnp.float32)) * scale
                up = (acc[k, rows, late] + recv[h, k, :, late].astype(jnp.float32)) * scale
                hid[k, :, at] = (gate / (1.0 + jnp.exp(-gate)) * up).astype(jnp.bfloat16)
            for cc in range(n_col):
                for dd in range(dests):
                    own_block = mine(h, dd, cc)
                    if own_block is False:
                        hid_copy(h, k, dd, cc).start()
                    else:
                        @pl.when(own_block)
                        def _():
                            index = cc * dests + dd
                            out[:, pl.ds(pl.multiple_of(c * width + k * tu, tu), tu)] = hid[
                                k, index * out_rows:(index + 1) * out_rows, :]

                        @pl.when(jnp.logical_not(own_block))
                        def _():
                            hid_copy(h, k, dd, cc).start()

    @pl.loop(0, tiles + (n - 1) * LAG)
    def _(s):
        @pl.when(s < tiles)
        def _():
            for copy in weight_copies(s):
                copy.wait()
            acc[s, :, :tu] = jnp.dot(scaled[...], gate_v[s], preferred_element_type=jnp.float32)
            acc[s, :, tu:] = jnp.dot(scaled[...], up_v[s], preferred_element_type=jnp.float32)

        for h in range(2):
            k = s - hop(h) * LAG

            @pl.when((k >= 0) & (k < tiles))
            def _():
                handle(h, k)

    for db in range(1, n_ba):
        to_chip(db).wait_send()
    for db in range(n_ba):
        for dc in range(1, n_col):
            to_core(db, dc).wait_send()
    for h in range(2):
        @pl.when(a != h * (n - 1))
        def _():
            sq_copy(h, a).wait_send()

    finisher = (a == 0) | (a == n - 1)

    @pl.loop(0, tiles)
    def _(k):
        for h in range(2):
            @pl.when(hop(h) < n - 1)
            def _():
                part_copy(h, k).wait_send()

            @pl.when(hop(h) == n - 1)
            def _():
                for cc in range(n_col):
                    for dd in range(dests):
                        @pl.when(jnp.logical_not(mine(h, dd, cc)))
                        def _():
                            hid_copy(h, k, dd, cc).wait_send()

        for cc in range(n_col):
            @pl.when(jnp.logical_not(finisher & (c == cc)))
            def _():
                spot = out.at[:, pl.ds(pl.multiple_of(cc * width + k * tu, tu), tu)]
                pltpu.make_async_remote_copy(
                    hid.at[k, pl.ds(0, out_rows)], spot, hid_send.at[k, 0], out_recv.at[k, cc],
                    device_id={"col": cc}, device_id_type=MESH).wait_recv()


def shards(sizes, tokens, norm_gain, gate_weight, up_weight):
    n, n_ba, n_col, tiles = sizes
    own_rows, depth = tokens.shape
    width = gate_weight.shape[1]
    tu = width // tiles
    rows = own_rows * n_ba * n_col
    half = rows // 2
    out_rows = rows // (n * n_col)
    bf16, f32 = jnp.bfloat16, jnp.float32
    dma = pltpu.SemaphoreType.DMA
    any_space = pl.BlockSpec(memory_space=pl.ANY)
    vmem = pl.BlockSpec(memory_space=pltpu.VMEM)
    flops = 2 * rows * depth * 2 * width
    return pl.pallas_call(
        functools.partial(kernel, sizes),
        out_shape=jax.ShapeDtypeStruct((out_rows, width * n_col), bf16),
        in_specs=[any_space, vmem, any_space, any_space],
        out_specs=vmem,
        scratch_shapes=[
            pltpu.VMEM((rows, depth), bf16),
            pltpu.VMEM((rows, depth), bf16),
            pltpu.VMEM((tiles, depth, tu), bf16),
            pltpu.VMEM((tiles, depth, tu), bf16),
            pltpu.VMEM((tiles, rows, 2 * tu), f32),
            pltpu.VMEM((2, tiles, half, 2 * tu), bf16),
            pltpu.VMEM((2, tiles, half, 2 * tu), bf16),
            pltpu.VMEM((tiles, half, tu), bf16),
            pltpu.VMEM((2, half // 128, 8, 128), f32),
            pltpu.VMEM((n, half // 128, 8, 128), f32),
            pltpu.VMEM((half, 128), f32),
            dma((2, tiles)),
            dma,
            dma((n_ba,)),
            dma((n_ba,)),
            dma((n_ba, n_col)),
            dma((n_ba, n_col)),
            dma((2, tiles)),
            dma((2, tiles)),
            dma((2,)),
            dma((n,)),
            dma((tiles, n // 2 * n_col)),
            dma((tiles, n_col)),
        ],
        compiler_params=pltpu.CompilerParams(
            collective_id=0, has_side_effects=True, vmem_limit_bytes=60 * 1024 * 1024),
        cost_estimate=pl.CostEstimate(
            flops=flops, bytes_accessed=4 * depth * width, transcendentals=half * width),
    )(tokens, norm_gain.reshape(1, depth), gate_weight, up_weight)


def solution(mesh):
    def run(tokens, norm_gain, gate_weight, up_weight):
        n, n_ba, n_col = mesh.shape["aa"], mesh.shape["ba"], mesh.shape["col"]
        width = gate_weight.shape[1] // (n_ba * n_col)
        tu = 256 if width % 256 == 0 and width > 1024 else 128
        sizes = (n, n_ba, n_col, width // tu)
        return jax.shard_map(
            functools.partial(shards, sizes),
            mesh=mesh,
            in_specs=(
                P(("groups", "col", "ba"), "aa"),
                P("aa"),
                P("aa", ("ba", "col")),
                P("aa", ("ba", "col")),
            ),
            out_specs=P(("groups", "col", "aa"), "ba"),
            check_vma=False,
        )(tokens, norm_gain, gate_weight, up_weight)

    return run
```

time: 202 us -> 79.4 us (0.39)
  waiting for transfers between devices: 136 us -> 0 us
  Pallas kernels: 0 us -> 75.5 us
  matrix products: 27.2 us -> 0 us
  blocking collectives: 20.5 us -> 0 us
  between operations: 13.2 us -> 0.01 us
  other arithmetic: 4.66 us -> 0 us
  local copies, waits for them, and re-layouts: 0.14 us -> 3.11 us
    pallas_call x0 -> x1, Pallas kernels: none -> 75.5 us  [shards(): pl.pallas_call(functools.partial(kernel, sizes), out_shape=jax.ShapeDtype...]
    reduce_scatter x1 -> x0, waiting for transfers between devices: 69.7 us -> none  [shards(): lax.psum_scatter(make_term(normed, gate_full, up_full).astype(jnp.bfloat1...]
    all_gather x2 -> x0, waiting for transfers between devices: 65 us -> none  [the longest x1 35.6 us: shards(): lax.all_gather(gate_weight, 'col', axis=1, tiled=True)]
    dot_general x2 -> x0, matrix products: 27.2 us -> none  [the longest x1 13.9 us: make_term(): up_part = jnp.dot(normed, up_block, preferred_element_type=jnp.float32)]
    psum x1 -> x0, blocking collectives: 13.5 us -> none  [shards(): totals = lax.psum(squares(tokens), 'aa')]
    all_gather x1 -> x0, blocking collectives: 7.05 us -> none  [gather_rows(): return lax.all_gather(local_rows, 'ba', axis=0, tiled=True)]
    convert_element_type x4 -> x0, other arithmetic: 2.46 us -> none  [the longest x1 1.3 us: shards(): summed = lax.psum_scatter(make_term(normed, gate_full, up_full).astype(jn...]
    concatenate x1 -> x0, other arithmetic: 2.04 us -> none  [make_term(): return jnp.concatenate([gate_part, up_part], axis=1)]
  transfers between devices with their start and end apart: 3 -> 0, of which waited for: 3 -> 0; matrix products, arithmetic and copies ran while one was open for 7% -> 0% of each run, Pallas kernels for 0% -> 0%
where the time goes in v1:
time: 79.4 us; the launch traced here: 78.6 us
  Pallas kernels  75.5 us (95%)
  local copies, waits for them, and re-layouts  3.11 us (4%)
    pallas_call x1, Pallas kernels, shards(): pl.pallas_call(functools.partial(kernel, sizes), out_shape=jax.ShapeDtype...  75.5 us
    unnamed x1, local copies, waits for them, and re-layouts  1.82 us

profile of v1, /device:TPU:0, one launch (start us, length us, event | category | flops | bytes accessed | tf_op | source)
XLA Modules:
  0.0 78.6 jit_solution(4155934689582751723)
XLA Ops:
  0.0 1.3 %reshape.3.gain = bf16[1,2048]{1,0:T(2,128)(2,1)} reshape(bf16[2048]{0:T(1024)(128)(2,1)} %param.5) | data formatting | bytes 8192 | tf_op jit(solution)/shard_map/reshape | solution.py:298
  1.3 75.5 %shard_map.46 = bf16[32,7168]{1,0:T(8,128)(2,1)} custom-call(bf16[64,2048]{1,0:T(8,128)(2,1)} %tokens.1, bf16[1,2048]{1,0:T(2,128)(2,1)} %reshape.3.gain, bf16[2048,3584]{1,0:T(8,128)(2,1)} %gate_w.1, bf16[2048,3584]{1,0:T(8,128)(2,1)} %up_w.1), custom_call_target="tpu_custom_call" | custom-call | flops 7516192768 | bytes 29360128 | tf_op jit(solution)/shard_map/pallas_call | solution.py:264
  76.8 1.8 %copy.6 = bf16[32,7168]{1,0:T(8,128)(2,1)} copy(bf16[32,7168]{1,0:T(8,128)(2,1)} %shard_map.46) | data formatting | bytes 917504

commit v2 on v1

v2 whole, which is shorter than its diff:
```python
import functools

import jax
import jax.numpy as jnp
from jax import lax
from jax.experimental import pallas as pl
from jax.experimental.pallas import tpu as pltpu
from jax.sharding import PartitionSpec as P

MESH = pl.DeviceIdType.MESH
EPSILON = 1e-05
LAG = 2
AHEAD = 6


def kernel(sizes, tokens, gain, gate_w, up_w, out, raw, scaled, gate_v, up_v, acc, recv, send,
           hid, sq_own, sq_recv, factor, w_sem, own_sem, x_send, x_recv, c_send, c_recv,
           part_send, part_recv, sq_send, sq_rsem, hid_send, out_recv):
    n, n_ba, n_col, tiles = sizes
    a, b, c = lax.axis_index("aa"), lax.axis_index("ba"), lax.axis_index("col")
    own_rows, depth = tokens.shape
    width = gate_w.shape[1]
    tu = width // tiles
    half = scaled.shape[0] // 2
    out_rows = out.shape[0]
    dests = n // 2
    ahead = min(AHEAD, tiles)
    late = tiles - 3 if n > 2 else tiles

    def start_of(bb, cc):
        per_half = n_ba // 2
        row = (bb // per_half) * half + cc * (half // n_col) + (bb % per_half) * own_rows
        return pl.multiple_of(row, own_rows)

    def block(bb, cc):
        return raw.at[pl.ds(start_of(bb, cc), own_rows)]

    def weight_copies(j):
        cols = pl.ds(pl.multiple_of(j * tu, tu), tu)
        return (pltpu.make_async_copy(gate_w.at[:, cols], gate_v.at[j], w_sem.at[0, j]),
                pltpu.make_async_copy(up_w.at[:, cols], up_v.at[j], w_sem.at[1, j]))

    barrier = pltpu.get_barrier_semaphore()
    peers = 0
    for da in range(n):
        for dc in range(n_col):
            if da or dc:
                pl.semaphore_signal(
                    barrier, inc=1, device_id_type=MESH,
                    device_id={"aa": lax.rem(a + da, n), "col": lax.rem(c + dc, n_col)})
                peers += 1
    for db in range(1, n_ba):
        pl.semaphore_signal(barrier, inc=1, device_id={"ba": lax.rem(b + db, n_ba)},
                            device_id_type=MESH)
        peers += 1

    own = pltpu.make_async_copy(tokens, block(b, c), own_sem)
    own.start()

    @pl.loop(0, tiles)
    def _(j):
        for copy in weight_copies(j):
            copy.start()

    pl.semaphore_wait(barrier, peers)

    def piece(ref, p):
        return ref.at[pl.ds(p * (own_rows // 2), own_rows // 2)]

    def back(i, d, count):
        return lax.rem(i - d + count, count)

    def to_chip(db, p, source=None):
        spot = block(b if source is None else source, c)
        return pltpu.make_async_remote_copy(
            piece(tokens, p), piece(spot, p), x_send.at[db, p], x_recv.at[db, p],
            device_id={"ba": lax.rem(b + db, n_ba)}, device_id_type=MESH)

    def to_core(db, dc, p):
        spot = piece(block(back(b, db, n_ba), c), p)
        return pltpu.make_async_remote_copy(
            piece(tokens, p) if db == 0 else spot, spot, c_send.at[db, dc, p],
            c_recv.at[db, dc, p],
            device_id={"col": lax.rem(c + dc, n_col)}, device_id_type=MESH)

    def from_core(db, dc, p):
        spot = piece(block(back(b, db, n_ba), back(c, dc, n_col)), p)
        return pltpu.make_async_remote_copy(
            piece(tokens, p), spot, c_send.at[db, dc, p], c_recv.at[db, dc, p],
            device_id={"col": lax.rem(c + dc, n_col)}, device_id_type=MESH)

    def forward(p):
        for db in range(1, n_ba):
            to_chip(db, p, back(b, db, n_ba)).wait_recv()
            for dc in range(1, n_col):
                to_core(db, dc, p).start()

    def arrive(dbs):
        for db in dbs:
            for dc in range(1, n_col):
                for p in range(2):
                    from_core(db, dc, p).wait_recv()

    def apply_gain(h):
        @pl.loop(0, half // 64)
        def _(r):
            rows = pl.ds(pl.multiple_of(h * half + r * 64, 64), 64)
            for q in range(depth // 128):
                cols = slice(q * 128, (q + 1) * 128)
                scaled[rows, cols] = (raw[rows, cols].astype(jnp.float32) * gain[:, cols].astype(
                    jnp.float32)).astype(jnp.bfloat16)

    def sq_copy(h, slot):
        return pltpu.make_async_remote_copy(
            sq_own.at[h], sq_recv.at[slot], sq_send.at[h], sq_rsem.at[slot],
            device_id={"aa": h * (n - 1)}, device_id_type=MESH)

    def squares(h):
        @pl.loop(0, half // 128)
        def _(r):
            rows = pl.ds(pl.multiple_of(h * half + r * 128, 128), 128)
            total = jnp.zeros((128, 128), jnp.float32)
            for q in range(depth // 128):
                value = raw[rows, q * 128:(q + 1) * 128].astype(jnp.float32)
                total = total + value * value
            line = jnp.sum(jnp.transpose(total), axis=0, keepdims=True)
            sq_own[h, r] = jnp.broadcast_to(line, (8, 128))

        @pl.when(a != h * (n - 1))
        def _():
            sq_copy(h, a).start()

    def hop(h):
        return jnp.where(h == 0, n - 1 - a, a)

    sub = half // n_col

    def part_copy(h, k, cc):
        to = jnp.where(h == 0, jnp.maximum(a - 1, 0), jnp.minimum(a + 1, n - 1))
        rows = pl.ds(cc * sub, sub)
        return pltpu.make_async_remote_copy(
            send.at[h, k, rows], recv.at[h, k, rows], part_send.at[h, k, cc],
            part_recv.at[h, k, cc], device_id={"aa": to}, device_id_type=MESH)

    def multiply(h, j):
        left = scaled[pl.ds(pl.multiple_of(h * half, half), half), :]
        acc[h, j, :, :tu] = jnp.dot(left, gate_v[j], preferred_element_type=jnp.float32)
        acc[h, j, :, tu:] = jnp.dot(left, up_v[j], preferred_element_type=jnp.float32)

        @pl.when(hop(h) == 0)
        def _():
            for cc in range(n_col):
                rows = slice(cc * sub, (cc + 1) * sub)
                send[h, j, rows, :] = acc[h, j, rows, :].astype(jnp.bfloat16)
                part_copy(h, j, cc).start()

    def hid_copy(h, dd, cc, i):
        index = cc * dests + dd
        first, count = (0, late) if i == 0 else (late + i - 1, 1)
        from_cols = pl.ds(first * tu, count * tu)
        to_cols = pl.ds(pl.multiple_of(c * width + first * tu, tu), count * tu)
        return pltpu.make_async_remote_copy(
            hid.at[pl.ds(index * out_rows, out_rows), from_cols], out.at[:, to_cols],
            hid_send.at[index, i], out_recv.at[c, i],
            device_id={"aa": h * dests + dd, "col": cc}, device_id_type=MESH)

    def elsewhere(h, dd, cc):
        return (a != h * dests + dd) | (c != cc)

    def send_hidden(h, i):
        for dd in range(dests):
            for cc in range(n_col):
                @pl.when(elsewhere(h, dd, cc))
                def _():
                    hid_copy(h, dd, cc, i).start()

    def find_factor(h):
        total = sq_own[h]
        for off in range(1, n):
            d = lax.rem(a + off, n)
            sq_copy(h, d).wait_recv()
            total = total + sq_recv[d]
        rate = lax.rsqrt(total / (depth * n) + EPSILON)
        for r in range(half // 128):
            factor[r * 128:(r + 1) * 128, :] = jnp.transpose(
                jnp.broadcast_to(rate[r, 0:1, :], (128, 128)))

    def finish(h, k, cc):
        rows = slice(cc * sub, (cc + 1) * sub)
        scale = factor[rows, :]
        for q in range(tu // 128):
            at = slice(q * 128, (q + 1) * 128)
            up_at = slice(tu + q * 128, tu + (q + 1) * 128)
            gate = (acc[h, k, rows, at] + recv[h, k, rows, at].astype(jnp.float32)) * scale
            up = (acc[h, k, rows, up_at] + recv[h, k, rows, up_at].astype(jnp.float32)) * scale
            cols = pl.ds(pl.multiple_of(k * tu + q * 128, 128), 128)
            hid[rows, cols] = (gate / (1.0 + jnp.exp(-gate)) * up).astype(jnp.bfloat16)

    def handle(h, k):
        here = hop(h)

        @pl.when((here > 0) & (here < n - 1))
        def _():
            for cc in range(n_col):
                part_copy(h, k, cc).wait_recv()
                rows = slice(cc * sub, (cc + 1) * sub)
                send[h, k, rows, :] = (
                    acc[h, k, rows, :] + recv[h, k, rows, :].astype(jnp.float32)
                ).astype(jnp.bfloat16)
                part_copy(h, k, cc).start()

        @pl.when(here == n - 1)
        def _():
            @pl.when(k == 0)
            def _():
                find_factor(h)

            for cc in range(n_col):
                part_copy(h, k, cc).wait_recv()
                finish(h, k, cc)

            @pl.when(k == late - 1)
            def _():
                @pl.loop(0, tiles)
                def _(j):
                    for cc in range(n_col):
                        part_copy(1 - h, j, cc).wait_send()

                send_hidden(h, 0)

            for i in range(1, tiles - late + 1):
                @pl.when(k == late + i - 1)
                def _():
                    send_hidden(h, i)

    near = b // (n_ba // 2)
    far = 1 - near

    for p in range(2):
        for db in range(1, n_ba):
            to_chip(db, p).start()
        for dc in range(1, n_col):
            to_core(0, dc, p).start()
    own.wait()
    if n_ba > 2:
        for p in range(2):
            forward(p)
        arrive(range(n_ba))
    else:
        arrive([0])
    apply_gain(near)

    @pl.loop(0, ahead)
    def _(j):
        for copy in weight_copies(j):
            copy.wait()
        multiply(near, j)
        if n_ba == 2:
            for p in range(2):
                @pl.when(j == (p + 1) * ahead // 2 - 1)
                def _():
                    forward(p)

    squares(near)
    if n_ba == 2:
        arrive([1])
    apply_gain(far)

    @pl.loop(0, tiles + (n - 1) * LAG)
    def _(s):
        @pl.when(s < tiles)
        def _():
            multiply(far, s)

        @pl.when(s == 0)
        def _():
            squares(far)

        @pl.when(s + ahead < tiles)
        def _():
            for copy in weight_copies(s + ahead):
                copy.wait()
            multiply(near, s + ahead)

        for h, k in ((near, s - (hop(near) - 1) * LAG), (far, s - hop(far) * LAG)):
            @pl.when((k >= 0) & (k < tiles) & (hop(h) > 0))
            def _():
                handle(h, k)

    finisher = (a == 0) | (a == n - 1)

    @pl.when(finisher)
    def _():
        ours = c * dests + jnp.where(a == 0, 0, dests - 1)
        out[:, pl.ds(pl.multiple_of(c * width, tu), width)] = hid[
            pl.ds(pl.multiple_of(ours * out_rows, out_rows), out_rows), :]
        side = jnp.where(a == 0, 0, 1)
        for dd in range(dests):
            for cc in range(n_col):
                @pl.when(elsewhere(side, dd, cc))
                def _():
                    for i in range(tiles - late + 1):
                        hid_copy(side, dd, cc, i).wait_send()

    @pl.when(jnp.logical_not(finisher))
    def _():
        @pl.loop(0, tiles)
        def _(k):
            for h in range(2):
                for cc in range(n_col):
                    part_copy(h, k, cc).wait_send()

    for p in range(2):
        for db in range(1, n_ba):
            to_chip(db, p).wait_send()
        for db in range(n_ba):
            for dc in range(1, n_col):
                to_core(db, dc, p).wait_send()
    for h in range(2):
        @pl.when(a != h * (n - 1))
        def _():
            sq_copy(h, a).wait_send()

    for cc in range(n_col):
        @pl.when(jnp.logical_not(finisher & (c == cc)))
        def _():
            for i in range(tiles - late + 1):
                first, count = (0, late) if i == 0 else (late + i - 1, 1)
                pltpu.make_async_remote_copy(
                    hid.at[pl.ds(0, out_rows), pl.ds(0, count * tu)],
                    out.at[:, pl.ds(cc * width + first * tu, count * tu)],
                    hid_send.at[0, i], out_recv.at[cc, i],
                    device_id={"col": cc}, device_id_type=MESH).wait_recv()


def shards(sizes, tokens, norm_gain, gate_weight, up_weight):
    n, n_ba, n_col, tiles = sizes
    own_rows, depth = tokens.shape
    width = gate_weight.shape[1]
    tu = width // tiles
    rows = own_rows * n_ba * n_col
    half = rows // 2
    out_rows = rows // (n * n_col)
    bf16, f32 = jnp.bfloat16, jnp.float32
    dma = pltpu.SemaphoreType.DMA
    any_space = pl.BlockSpec(memory_space=pl.ANY)
    vmem = pl.BlockSpec(memory_space=pltpu.VMEM)
    flops = 2 * rows * depth * 2 * width
    return pl.pallas_call(
        functools.partial(kernel, sizes),
        out_shape=jax.ShapeDtypeStruct((out_rows, width * n_col), bf16),
        in_specs=[any_space, vmem, any_space, any_space],
        out_specs=vmem,
        scratch_shapes=[
            pltpu.VMEM((rows, depth), bf16),
            pltpu.VMEM((rows, depth), bf16),
            pltpu.VMEM((tiles, depth, tu), bf16),
            pltpu.VMEM((tiles, depth, tu), bf16),
            pltpu.VMEM((2, tiles, half, 2 * tu), f32),
            pltpu.VMEM((2, tiles, half, 2 * tu), bf16),
            pltpu.VMEM((2, tiles, half, 2 * tu), bf16),
            pltpu.VMEM((half, width), bf16),
            pltpu.VMEM((2, half // 128, 8, 128), f32),
            pltpu.VMEM((n, half // 128, 8, 128), f32),
            pltpu.VMEM((half, 128), f32),
            dma((2, tiles)),
            dma,
            dma((n_ba, 2)),
            dma((n_ba, 2)),
            dma((n_ba, n_col, 2)),
            dma((n_ba, n_col, 2)),
            dma((2, tiles, n_col)),
            dma((2, tiles, n_col)),
            dma((2,)),
            dma((n,)),
            dma((n // 2 * n_col, 4)),
            dma((n_col, 4)),
        ],
        compiler_params=pltpu.CompilerParams(
            collective_id=0, has_side_effects=True, vmem_limit_bytes=60 * 1024 * 1024),
        cost_estimate=pl.CostEstimate(
            flops=flops, bytes_accessed=4 * depth * width, transcendentals=half * width),
    )(tokens, norm_gain.reshape(1, depth), gate_weight, up_weight)


def solution(mesh):
    def run(tokens, norm_gain, gate_weight, up_weight):
        n, n_ba, n_col = mesh.shape["aa"], mesh.shape["ba"], mesh.shape["col"]
        width = gate_weight.shape[1] // (n_ba * n_col)
        tu = 256 if width % 256 == 0 and width > 1024 else 128
        sizes = (n, n_ba, n_col, width // tu)
        return jax.shard_map(
            functools.partial(shards, sizes),
            mesh=mesh,
            in_specs=(
                P(("groups", "col", "ba"), "aa"),
                P("aa"),
                P("aa", ("ba", "col")),
                P("aa", ("ba", "col")),
            ),
            out_specs=P(("groups", "col", "aa"), "ba"),
            check_vma=False,
        )(tokens, norm_gain, gate_weight, up_weight)

    return run
```

time: 79.4 us -> 72.2 us (0.909)
  Pallas kernels: 75.5 us -> 68.5 us
    pallas_call x1, Pallas kernels: 75.5 us -> 68.5 us  [shards(): pl.pallas_call(functools.partial(kernel, sizes), out_shape=jax.ShapeDtype...]
where the time goes in v2:
time: 72.2 us; the launch traced here: 71.6 us
  Pallas kernels  68.5 us (95%)
  local copies, waits for them, and re-layouts  3.11 us (4%)
    pallas_call x1, Pallas kernels, shards(): pl.pallas_call(functools.partial(kernel, sizes), out_shape=jax.ShapeDtype...  68.5 us
    unnamed x1, local copies, waits for them, and re-layouts  1.82 us

profile of v2, /device:TPU:0, one launch (start us, length us, event | category | flops | bytes accessed | tf_op | source)
XLA Modules:
  0.0 71.6 jit_solution(12265583405557074535)
XLA Ops:
  0.0 1.3 %reshape.3.gain = bf16[1,2048]{1,0:T(2,128)(2,1)} reshape(bf16[2048]{0:T(1024)(128)(2,1)} %param.5) | data formatting | bytes 8192 | tf_op jit(solution)/shard_map/reshape | solution.py:383
  1.3 68.5 %shard_map.46 = bf16[32,7168]{1,0:T(8,128)(2,1)} custom-call(bf16[64,2048]{1,0:T(8,128)(2,1)} %tokens.1, bf16[1,2048]{1,0:T(2,128)(2,1)} %reshape.3.gain, bf16[2048,3584]{1,0:T(8,128)(2,1)} %gate_w.1, bf16[2048,3584]{1,0:T(8,128)(2,1)} %up_w.1), custom_call_target="tpu_custom_call" | custom-call | flops 7516192768 | bytes 29360128 | tf_op jit(solution)/shard_map/pallas_call | solution.py:349
  69.8 1.8 %copy.6 = bf16[32,7168]{1,0:T(8,128)(2,1)} copy(bf16[32,7168]{1,0:T(8,128)(2,1)} %shard_map.46) | data formatting | bytes 917504

commit v3 on v2

--- a/solution.py
+++ b/solution.py
@@ -9,7 +9,6 @@
 
 MESH = pl.DeviceIdType.MESH
 EPSILON = 1e-05
-LAG = 2
 AHEAD = 6
 
 
@@ -107,7 +106,7 @@
             rows = pl.ds(pl.multiple_of(h * half + r * 64, 64), 64)
             for q in range(depth // 128):
                 cols = slice(q * 128, (q + 1) * 128)
-                scaled[rows, cols] = (raw[rows, cols].astype(jnp.float32) * gain[:, cols].astype(
+                scaled[rows, cols] = (raw[rows, cols].astype(jnp.float32) * gain[cols].astype(
                     jnp.float32)).astype(jnp.bfloat16)
 
     def sq_copy(h, slot):
@@ -235,6 +234,8 @@
 
     near = b // (n_ba // 2)
     far = 1 - near
+    near_lag = hop(near) - 1 + jnp.where(hop(near) == n - 1, 2, 0)
+    far_lag = jnp.where(hop(far) == 0, 0, 2 * hop(far) - 1)
 
     for p in range(2):
         for db in range(1, n_ba):
@@ -266,7 +267,7 @@
         arrive([1])
     apply_gain(far)
 
-    @pl.loop(0, tiles + (n - 1) * LAG)
+    @pl.loop(0, tiles + 2 * n)
     def _(s):
         @pl.when(s < tiles)
         def _():
@@ -282,7 +283,7 @@
                 copy.wait()
             multiply(near, s + ahead)
 
-        for h, k in ((near, s - (hop(near) - 1) * LAG), (far, s - hop(far) * LAG)):
+        for h, k in ((near, s - near_lag), (far, s - far_lag)):
             @pl.when((k >= 0) & (k < tiles) & (hop(h) > 0))
             def _():
                 handle(h, k)
@@ -380,7 +381,7 @@
             collective_id=0, has_side_effects=True, vmem_limit_bytes=60 * 1024 * 1024),
         cost_estimate=pl.CostEstimate(
             flops=flops, bytes_accessed=4 * depth * width, transcendentals=half * width),
-    )(tokens, norm_gain.reshape(1, depth), gate_weight, up_weight)
+    )(tokens, norm_gain, gate_weight, up_weight)
 
 
 def solution(mesh):

time: 72.2 us -> 70.5 us (0.976)
  local copies, waits for them, and re-layouts: 3.11 us -> 1.82 us
    reshape x1 -> x0, local copies, waits for them, and re-layouts: 1.29 us -> none  [shards(): norm_gain.reshape(1, depth)]
where the time goes in v3:
time: 70.5 us; the launch traced here: 70.3 us
  Pallas kernels  68.5 us (97%)
  local copies, waits for them, and re-layouts  1.82 us (3%)
    pallas_call x1, Pallas kernels, shards(): pl.pallas_call(functools.partial(kernel, sizes), out_shape=jax.ShapeDtype...  68.5 us
    unnamed x1, local copies, waits for them, and re-layouts  1.82 us

profile of v3, /device:TPU:0, one launch (start us, length us, event | category | flops | bytes accessed | tf_op | source)
XLA Modules:
  0.0 70.3 jit_solution(8401901819408481721)
XLA Ops:
  0.0 68.5 %shard_map.46 = bf16[32,7168]{1,0:T(8,128)(2,1)} custom-call(bf16[64,2048]{1,0:T(8,128)(2,1)} %tokens.1, bf16[2048]{0:T(1024)(128)(2,1)} %gain.1, bf16[2048,3584]{1,0:T(8,128)(2,1)} %gate_w.1, bf16[2048,3584]{1,0:T(8,128)(2,1)} %up_w.1), custom_call_target="tpu_custom_call" | custom-call | flops 7516192768 | bytes 29360128 | tf_op jit(solution)/shard_map/pallas_call | solution.py:350
  68.5 1.8 %copy.6 = bf16[32,7168]{1,0:T(8,128)(2,1)} copy(bf16[32,7168]{1,0:T(8,128)(2,1)} %shard_map.46) | data formatting | bytes 917504

commit v4 on v3

--- a/solution.py
+++ b/solution.py
@@ -262,7 +262,6 @@
                 def _():
                     forward(p)
 
-    squares(near)
     if n_ba == 2:
         arrive([1])
     apply_gain(far)
@@ -273,8 +272,9 @@
         def _():
             multiply(far, s)
 
-        @pl.when(s == 0)
-        def _():
+        @pl.when(s == 1)
+        def _():
+            squares(near)
             squares(far)
 
         @pl.when(s + ahead < tiles)

time: 70.5 us -> 71.1 us (level)
  no operation moved by 1% of the time
where the time goes in v4:
time: 71.1 us; the launch traced here: 70.7 us
  Pallas kernels  68.9 us (97%)
  local copies, waits for them, and re-layouts  1.82 us (3%)
    pallas_call x1, Pallas kernels, shards(): pl.pallas_call(functools.partial(kernel, sizes), out_shape=jax.ShapeDtype...  68.9 us
    unnamed x1, local copies, waits for them, and re-layouts  1.82 us

profile of v4, /device:TPU:0, one launch (start us, length us, event | category | flops | bytes accessed | tf_op | source)
XLA Modules:
  0.0 70.7 jit_solution(10479444824782538702)
XLA Ops:
  0.0 68.9 %shard_map.46 = bf16[32,7168]{1,0:T(8,128)(2,1)} custom-call(bf16[64,2048]{1,0:T(8,128)(2,1)} %tokens.1, bf16[2048]{0:T(1024)(128)(2,1)} %gain.1, bf16[2048,3584]{1,0:T(8,128)(2,1)} %gate_w.1, bf16[2048,3584]{1,0:T(8,128)(2,1)} %up_w.1), custom_call_target="tpu_custom_call" | custom-call | flops 7516192768 | bytes 29360128 | tf_op jit(solution)/shard_map/pallas_call | solution.py:350
  68.9 1.8 %copy.6 = bf16[32,7168]{1,0:T(8,128)(2,1)} copy(bf16[32,7168]{1,0:T(8,128)(2,1)} %shard_map.46) | data formatting | bytes 917504
